TPU v7x, 32 devices: a whole 2x2x4 slice. The times are simulated.
32 devices in a mesh: band: 16 (over z, y, core), batch: 2 (over x).
Axes of the slice: x: 2, y: 2, z: 4, core: 2. Of those that a mesh axis runs over, the one named last changes fastest.
Arguments:
- tokens_in: bfloat16 [2, 2, 112, 112, 256], P(None, 'batch', 'band'), may hold values from -6 to 6
- cotangent: bfloat16 [2, 2, 112, 112, 256], P(None, 'batch', 'band'), may hold values from -6 to 6
- owners: int32 [4], replicated, may hold values from 0 to 31
- weight_qkv: float32 [32, 256, 768], P(('band', 'batch')), may hold values from -0.375 to 0.375
- weight_proj: float32 [32, 256, 256], P(('band', 'batch')), may hold values from -0.75 to 0.75
- weight_fc1: float32 [32, 256, 1024], P(('band', 'batch')), may hold values from -0.375 to 0.375
- weight_fc2: float32 [32, 1024, 256], P(('band', 'batch')), may hold values from -0.1875 to 0.1875
- first_qkv: float32 [32, 256, 768], P(('band', 'batch')), may hold values from -384 to 384
- second_qkv: float32 [32, 256, 768], P(('band', 'batch')), may hold values from 3010.56 to 12042.24
- first_proj: float32 [32, 256, 256], P(('band', 'batch')), may hold values from -384 to 384
- second_proj: float32 [32, 256, 256], P(('band', 'batch')), may hold values from 3010.56 to 12042.24
- first_fc1: float32 [32, 256, 1024], P(('band', 'batch')), may hold values from -384 to 384
- second_fc1: float32 [32, 256, 1024], P(('band', 'batch')), may hold values from 3010.56 to 12042.24
- first_fc2: float32 [32, 1024, 256], P(('band', 'batch')), may hold values from -384 to 384
- second_fc2: float32 [32, 1024, 256], P(('band', 'batch')), may hold values from 3010.56 to 12042.24
- left_qkv: float32 [256, 256], replicated, may hold values from -1 to 1, as said below
- right_qkv: float32 [768, 768], replicated, may hold values from -1 to 1, as said below
- left_proj: float32 [256, 256], replicated, may hold values from -1 to 1, as said below
- right_proj: float32 [256, 256], replicated, may hold values from -1 to 1, as said below
- left_fc1: float32 [256, 256], replicated, may hold values from -1 to 1, as said below
- right_fc1: float32 [1024, 1024], replicated, may hold values from -1 to 1, as said below
- left_fc2: float32 [1024, 1024], replicated, may hold values from -1 to 1, as said below
- right_fc2: float32 [256, 256], replicated, may hold values from -1 to 1, as said below
- vectors: float32 [22, 256], replicated, may hold values from -0.5 to 1.5, as said below
- vectors_first: float32 [22, 256], replicated, may hold values from -384 to 384
- vectors_second: float32 [22, 256], replicated, may hold values from 3010.56 to 12042.24
Outputs:
- block_out: bfloat16 [2, 2, 112, 112, 256], P(None, 'batch', 'band')
- input_grad: bfloat16 [2, 2, 112, 112, 256], P(None, 'batch', 'band')
- grad_qkv: float32 [256, 768], replicated
- first_new_qkv: float32 [32, 256, 768], P(('band', 'batch'))
- second_new_qkv: float32 [32, 256, 768], P(('band', 'batch'))
- weight_new_qkv: float32 [32, 256, 768], P(('band', 'batch'))
- grad_proj: float32 [256, 256], replicated
- first_new_proj: float32 [32, 256, 256], P(('band', 'batch'))
- second_new_proj: float32 [32, 256, 256], P(('band', 'batch'))
- weight_new_proj: float32 [32, 256, 256], P(('band', 'batch'))
- grad_fc1: float32 [256, 1024], replicated
- first_new_fc1: float32 [32, 256, 1024], P(('band', 'batch'))
- second_new_fc1: float32 [32, 256, 1024], P(('band', 'batch'))
- weight_new_fc1: float32 [32, 256, 1024], P(('band', 'batch'))
- grad_fc2: float32 [1024, 256], replicated
- first_new_fc2: float32 [32, 1024, 256], P(('band', 'batch'))
- second_new_fc2: float32 [32, 1024, 256], P(('band', 'batch'))
- weight_new_fc2: float32 [32, 1024, 256], P(('band', 'batch'))
- vectors_grad: float32 [22, 256], replicated
- vectors_first_new: float32 [22, 256], replicated
- vectors_second_new: float32 [22, 256], replicated
- vectors_new: float32 [22, 256], replicated
Inputs may be any that keep to these rules, and one draw needn't show every extreme that they name: `left_qkv`: an orthogonal 256 x 256 matrix. `right_qkv`: an orthogonal 3 * 256 x 3 * 256 matrix. `left_proj`: an orthogonal 256 x 256 matrix. `right_proj`: an orthogonal 256 x 256 matrix. `left_fc1`: an orthogonal 256 x 256 matrix. `right_fc1`: an orthogonal 1024 x 1024 matrix. `left_fc2`: an orthogonal 1024 x 1024 matrix. `right_fc2`: an orthogonal 256 x 256 matrix. `vectors`: gains in rows 0 and 5 from 0.5 to 1.5, taps from -0.5 to 0.5, biases from -0.2 to 0.2.
All inputs are finite; a program needn't handle non-finite values.
Results may differ from a plain program's by a relative error of at most 0.011.
Values may be sent and summed in bfloat16 or wider, within the bound.
A program may use at most 512 MiB of HBM per device.

v0:
```python
import functools

import jax
import jax.numpy as jnp
from jax import lax
from jax.experimental import pallas as pl
from jax.experimental.pallas import tpu as pltpu
from jax.sharding import PartitionSpec as P

HEAD_DIM = 32
STRIPE = 7
STEP = 10
EPS_NORM = 1e-05
BETA_ONE = 0.5
BETA_TWO = 0.6
RATE = 0.04
RATE_VECTORS = 0.2
DECAY = 0.01
EPS_ADAM = 1e-08
MESH = pl.DeviceIdType.MESH
F32 = jnp.float32
BF16 = jnp.bfloat16
PIECE = 64
LOG2E = 1.4426950408889634
LN2 = 0.6931471805599453
Q_SCALE = LOG2E * HEAD_DIM**-0.5
LONGEST = 1024
VMEM_LIMIT = 60 * 1024 * 1024
ROW_QKV, ROW_PROJ, ROW_FC1, ROW_FC2, ROW_END = 0, 768, 1024, 2048, 3072


def mm(a, b):
    return lax.dot_general(a, b, (((1,), (0,)), ((), ())), preferred_element_type=F32)


def mm_nt(a, b):
    return lax.dot_general(a, b, (((1,), (1,)), ((), ())), preferred_element_type=F32)


def mm_tn(a, b):
    return lax.dot_general(a, b, (((0,), (0,)), ((), ())), preferred_element_type=F32)


def exchange_kernel(n, piece, x_ref, o_ref, send_sem, recv_sem, loc_sem):
    me = lax.axis_index("band")
    bar = pltpu.get_barrier_semaphore()

    def greet(k, c):
        pl.semaphore_signal(
            bar, inc=1, device_id={"band": lax.rem(me + k, n)}, device_id_type=MESH
        )
        return c

    lax.fori_loop(1, n, greet, 0)
    pl.semaphore_wait(bar, n - 1)

    def rows(i):
        return pl.ds(pl.multiple_of(i * piece, piece), piece)

    def send(k, c):
        d = lax.rem(me + k, n)
        pltpu.make_async_remote_copy(
            src_ref=x_ref.at[rows(d)],
            dst_ref=o_ref.at[rows(me)],
            send_sem=send_sem.at[k],
            recv_sem=recv_sem.at[k],
            device_id={"band": d},
            device_id_type=MESH,
        ).start()
        return c

    lax.fori_loop(1, n, send, 0)
    local = pltpu.make_async_copy(x_ref.at[rows(me)], o_ref.at[rows(me)], loc_sem)
    local.start()
    local.wait()

    def take(k, c):
        s = lax.rem(me - k + n, n)
        pltpu.make_async_remote_copy(
            src_ref=x_ref.at[rows(s)],
            dst_ref=o_ref.at[rows(s)],
            send_sem=send_sem.at[k],
            recv_sem=recv_sem.at[k],
            device_id={"band": s},
            device_id_type=MESH,
        ).wait()
        return c

    lax.fori_loop(1, n, take, 0)


def exchange(x, n, cid):
    return pl.pallas_call(
        functools.partial(exchange_kernel, n, x.shape[0] // n),
        out_shape=jax.ShapeDtypeStruct(x.shape, x.dtype),
        in_specs=[pl.BlockSpec(memory_space=pltpu.VMEM)],
        out_specs=pl.BlockSpec(memory_space=pltpu.VMEM),
        scratch_shapes=[
            pltpu.SemaphoreType.DMA((n,)),
            pltpu.SemaphoreType.DMA((n,)),
            pltpu.SemaphoreType.DMA,
        ],
        compiler_params=pltpu.CompilerParams(
            collective_id=cid, has_side_effects=True, vmem_limit_bytes=VMEM_LIMIT
        ),
        name="exchange",
    )(x)


def sum_kernel(nb, nx, total_rows, x_ref, o_ref, got, half, recv, s1, r1, s2, r2, s3, r3, s4, r4):
    nq = (nb // 2) * nx
    p = total_rows // (2 * nq)
    band = lax.axis_index("band")
    core = lax.rem(band, 2)
    q = (band // 2) * nx + lax.axis_index("batch")
    sibling = {"band": band + 1 - 2 * core}
    bar = pltpu.get_barrier_semaphore()

    def chip(t):
        return {"band": (t // nx) * 2 + core, "batch": lax.rem(t, nx)}

    def ahead(k):
        return lax.rem(q + k, nq)

    def behind(k):
        return lax.rem(q - k + nq, nq)

    def copy(src, dst, ss, rs, dev):
        return pltpu.make_async_remote_copy(
            src_ref=src, dst_ref=dst, send_sem=ss, recv_sem=rs, device_id=dev, device_id_type=MESH
        )

    def loop(lo, hi, body):
        def step(k, c):
            body(k)
            return c

        lax.fori_loop(lo, hi, step, 0)

    pl.semaphore_signal(bar, inc=1, device_id=sibling, device_id_type=MESH)
    loop(
        1,
        nq,
        lambda k: pl.semaphore_signal(
            bar, inc=1, device_id=chip(ahead(k)), device_id_type=MESH
        ),
    )
    pl.semaphore_wait(bar, nq)

    def whole_rows(c, t):
        return pl.ds(pl.multiple_of((c * nq + t) * p, 16), p)

    def half_rows(t):
        return pl.ds(pl.multiple_of(t * p, 16), p)

    def pair_copy(k, side):
        t = ahead(k)
        return copy(
            x_ref.at[whole_rows(side, t)], got.at[half_rows(t)], s1.at[t], r1.at[t], sibling
        )

    loop(1, nq + 1, lambda k: pair_copy(k, 1 - core).start())

    def scatter_copy(k):
        t = ahead(k)
        return copy(half.at[half_rows(t)], recv.at[half_rows(q)], s2.at[k], r2.at[k], chip(t))

    def pair_sum(k):
        t = ahead(k)
        pair_copy(k, core).wait()
        half[half_rows(t)] = (
            x_ref[whole_rows(core, t)].astype(F32) + got[half_rows(t)].astype(F32)
        ).astype(BF16)

        @pl.when(k < nq)
        def _():
            scatter_copy(k).start()

    loop(1, nq + 1, pair_sum)

    def add_piece(k, acc):
        t = behind(k)
        copy(half.at[half_rows(t)], recv.at[half_rows(t)], s2.at[k], r2.at[k], chip(t)).wait()
        return acc + recv[half_rows(t)].astype(F32)

    total = lax.fori_loop(1, nq, add_piece, half[half_rows(q)].astype(F32))
    mine = o_ref.at[whole_rows(core, q)]
    o_ref[whole_rows(core, q)] = total.astype(BF16)

    def gather_copy(k):
        return copy(mine, mine, s3.at[k], r3.at[k], chip(ahead(k)))

    def pass_on(t, side):
        return copy(
            o_ref.at[whole_rows(core, t)],
            o_ref.at[whole_rows(side, t)],
            s4.at[t],
            r4.at[t],
            sibling,
        )

    loop(1, nq, lambda k: gather_copy(k).start())
    pass_on(q, core).start()

    def relay(k):
        t = behind(k)
        copy(mine, o_ref.at[whole_rows(core, t)], s3.at[k], r3.at[k], chip(t)).wait()
        pass_on(t, core).start()

    loop(1, nq, relay)
    loop(0, nq, lambda t: pass_on(t, 1 - core).wait())


def sum_everywhere(x, nb, nx, cid):
    rows, cols = x.shape
    nq = nb // 2 * nx
    unit = 32 * nq
    padded = -(-rows // unit) * unit
    if padded != rows:
        x = jnp.concatenate([x, jnp.zeros((padded - rows, cols), x.dtype)], axis=0)
    sems = [pltpu.SemaphoreType.DMA((nq,)) for _ in range(8)]
    out = pl.pallas_call(
        functools.partial(sum_kernel, nb, nx, padded),
        out_shape=jax.ShapeDtypeStruct(x.shape, x.dtype),
        in_specs=[pl.BlockSpec(memory_space=pltpu.VMEM)],
        out_specs=pl.BlockSpec(memory_space=pltpu.VMEM),
        scratch_shapes=[pltpu.VMEM((padded // 2, cols), x.dtype)] * 3 + sems,
        compiler_params=pltpu.CompilerParams(
            collective_id=cid, has_side_effects=True, vmem_limit_bytes=VMEM_LIMIT
        ),
        name="sum_everywhere",
    )(x)
    return out


def order_out(pieces_n, length):
    row = lax.broadcasted_iota(jnp.int32, (pieces_n * PIECE, 1), 0)
    s = row // PIECE
    m = row % PIECE
    a = (m * 37) // 256
    b = m - STRIPE * a
    token = jnp.where(m < STRIPE * STRIPE, a * length + STRIPE * s + b, -1)
    column = lax.broadcasted_iota(jnp.int32, (pieces_n * PIECE, STRIPE * length), 1)
    return jnp.where(column == token, 1.0, 0.0).astype(BF16)


def order_in(pieces_n, length):
    row = lax.broadcasted_iota(jnp.int32, (1, pieces_n * PIECE), 1)
    s = row // PIECE
    m = row % PIECE
    a = (m * 37) // 256
    b = m - STRIPE * a
    token = jnp.where(m < STRIPE * STRIPE, b * length + STRIPE * s + a, -1)
    column = lax.broadcasted_iota(jnp.int32, (STRIPE * length, pieces_n * PIECE), 0)
    return jnp.where(column == token, 1.0, 0.0).astype(BF16)


def unit_rows(values):
    centred = values - jnp.mean(values, axis=-1, keepdims=True)
    inverse = lax.rsqrt(jnp.mean(centred * centred, axis=-1, keepdims=True) + EPS_NORM)
    return centred * inverse, inverse


def norm_back(grad_normed, gain, unit, inverse):
    scaled = grad_normed * gain
    first_mean = jnp.mean(scaled, axis=-1, keepdims=True)
    second_mean = jnp.mean(scaled * unit, axis=-1, keepdims=True)
    return inverse * (scaled - first_mean - unit * second_mean)


def shifted_columns(v, length):
    tokens = v.shape[0]
    column = lax.broadcasted_iota(jnp.int32, v.shape, 0) % length
    before = jnp.where(column == 0, 0.0, pltpu.roll(v, 1, 0))
    after = jnp.where(column == length - 1, 0.0, pltpu.roll(v, tokens - 1, 0))
    return before, v, after


def shifted_rows(v, length):
    zeros = jnp.zeros((length, v.shape[1]), v.dtype)
    above = jnp.concatenate([zeros, v[: v.shape[0] - length]], axis=0)
    below = jnp.concatenate([v[length:], zeros], axis=0)
    return above, v, below


def half_rows(vec_ref, half):
    def get(i):
        if 2 <= i < 11:
            a, b = divmod(i - 2, 3)
            row = 12 + (3 * a + b if half == 0 else 3 * b + a)
        else:
            row = {0: 2, 1: 3, 11: 21}[i]
        return vec_ref[row : row + 1, 128 * half : 128 * half + 128]

    return get


def conv(v, hv, length, flipped):
    total = jnp.zeros_like(v)
    for b, col in enumerate(shifted_columns(v, length)):
        for a, val in enumerate(shifted_rows(col, length)):
            total = total + val * hv(2 + (8 - 3 * a - b if flipped else 3 * a + b))
    return total


def head_mask(shape, h, offset=0):
    lane = lax.broadcasted_iota(jnp.int32, shape, len(shape) - 1) - offset
    return (lane >= h * HEAD_DIM) & (lane < (h + 1) * HEAD_DIM)


def three_parts(x):
    lane = lax.broadcasted_iota(jnp.int32, x.shape, len(x.shape) - 1) % HEAD_DIM
    hi = x.astype(BF16).astype(F32)
    mid = (x - hi).astype(BF16).astype(F32)
    low = x - hi - mid
    parts = jnp.where(lane == 0, hi, jnp.where(lane == 1, mid, jnp.where(lane == 2, low, 0.0)))
    return parts.astype(BF16)


def head_lanes(h, width):
    lane = lax.broadcasted_iota(jnp.int32, (1, width), 1) % 128
    keep = (lane >= h * HEAD_DIM) & (lane < (h + 1) * HEAD_DIM)
    return jnp.where(keep, 1.0, 0.0).astype(BF16)


def beside_parts(block):
    lane = lax.broadcasted_iota(jnp.int32, block.shape, 1) % HEAD_DIM
    return jnp.concatenate([block, jnp.where(lane < 3, 1.0, 0.0).astype(BF16)], axis=1)


def turned(block):
    return jnp.transpose(block.astype(F32)).astype(BF16)


def lane_blocks(w_ref, half):
    return lambda b: w_ref[256 * b : 256 * b + 256, 128 * half : 128 * half + 128]


def attention_forward(x, hv, length, wb, vec_ref, qa_ref, k_ref, v_ref, o_ref, att_ref):
    tokens = x.shape[0]
    unit, _ = unit_rows(x)
    normed = (unit * vec_ref[0:1] + vec_ref[1:2]).astype(BF16)
    qa_ref[:, 0:128] = ((mm(normed, wb(0)) + hv(0)) * Q_SCALE).astype(BF16)
    k_ref[...] = mm(normed, wb(1)).astype(BF16)
    v = (mm(normed, wb(2)) + hv(1)).astype(BF16)
    v_ref[...] = v

    def heads(v_turned, weighted, totals, tops):
        v_turned[...] = turned(v)

        def head_scores(h):
            return mm_nt(k_ref[...] * head_lanes(h, 128), qa_ref[:, 0:128])

        following = head_scores(0)
        ones = jnp.ones((HEAD_DIM, tokens), BF16)
        for h in range(4):
            scores = following
            if h < 3:
                following = head_scores(h + 1)
            highest = jnp.max(scores, axis=0, keepdims=True)
            probs = jnp.exp2(scores - highest).astype(BF16)
            rows = slice(HEAD_DIM * h, HEAD_DIM * h + HEAD_DIM)
            both = mm(jnp.concatenate([v_turned[rows, :], ones], axis=0), probs)
            weighted[rows, :] = both[:HEAD_DIM]
            totals[rows, :] = both[HEAD_DIM:]
            tops[rows, :] = jnp.broadcast_to(highest, (HEAD_DIM, tokens))

        o_ref[...] = jnp.transpose(weighted[...] / totals[...])
        log_total = tops[...] + jnp.log2(totals[...])
        qa_ref[:, 128:256] = three_parts(-jnp.transpose(log_total))

    pl.run_scoped(heads, pltpu.VMEM((128, tokens), BF16), *[pltpu.VMEM((128, tokens), F32)] * 3)
    lepe = conv(v_ref[...].astype(F32), hv, length, False)
    att_ref[...] = (o_ref[...] + lepe + hv(11)).astype(BF16)


def attention_backward(
    x, hv, length, grad, wb, vec_ref, qa_ref, k_ref, v_ref, o_ref, da_ref, gw_ref, rows_ref,
    between=None,
):
    tokens = x.shape[0]
    grad_f = grad.astype(F32)
    product = grad_f * o_ref[...]
    inner = jnp.zeros_like(product)
    for h in range(4):
        keep = head_mask(product.shape, h)
        inner = jnp.where(
            keep, jnp.sum(jnp.where(keep, product, 0.0), axis=-1, keepdims=True), inner
        )
    da_ref[:, 0:128] = grad
    da_ref[:, 128:256] = three_parts(-inner)

    def heads(k_turned, q_turned, grad_turned, k_wide, v_wide, dqs, dks, dvs):
        k_turned[...] = turned(k_ref[...])
        q_turned[...] = turned(qa_ref[:, 0:128])
        grad_turned[...] = turned(grad)
        k_wide[...] = beside_parts(k_ref[...])
        v_wide[...] = beside_parts(v_ref[...])

        def head_products(h):
            mask = head_lanes(h, 256)
            return mm_nt(qa_ref[...] * mask, k_wide[...]), mm_nt(da_ref[...] * mask, v_wide[...])

        early = tokens <= LONGEST
        following = head_products(0) if early else None
        for h in range(4):
            scores, grad_probs = following if early else head_products(h)
            if early and h < 3:
                following = head_products(h + 1)
            probs = jnp.exp2(scores)
            grad_scores = (probs * grad_probs).astype(BF16)
            rows = slice(HEAD_DIM * h, HEAD_DIM * h + HEAD_DIM)
            dvs[rows, :] = mm(grad_turned[rows, :], probs.astype(BF16))
            dks[rows, :] = mm(q_turned[rows, :], grad_scores)
            dqs[rows, :] = mm_nt(k_turned[rows, :], grad_scores)

        if between is not None:
            between()
        dq = (jnp.transpose(dqs[...]) * HEAD_DIM**-0.5).astype(BF16)
        dk = (jnp.transpose(dks[...]) * LN2).astype(BF16)
        dv = (jnp.transpose(dvs[...]) + conv(grad_f, hv, length, True)).astype(BF16)
        unit, _ = unit_rows(x)
        normed = (unit * vec_ref[0:1] + vec_ref[1:2]).astype(BF16)
        gw_ref[...] += mm_tn(normed, jnp.concatenate([dq, dk, dv], axis=1))
        rows_ref[0:1, :] += jnp.sum(dq.astype(F32), axis=0, keepdims=True)
        rows_ref[1:2, :] += jnp.sum(dv.astype(F32), axis=0, keepdims=True)
        for b, col in enumerate(shifted_columns(v_ref[...].astype(F32), length)):
            for a, val in enumerate(shifted_rows(col, length)):
                row = 2 + 3 * a + b
                rows_ref[row : row + 1, :] += jnp.sum(grad_f * val, axis=0, keepdims=True)
        rows_ref[11:12, :] += jnp.sum(grad_f, axis=0, keepdims=True)
        part = mm_nt(dq, wb(0)) + mm_nt(dk, wb(1)) + mm_nt(dv, wb(2))
        gain_row = jnp.sum(part * unit, axis=0, keepdims=True)
        shift_row = jnp.sum(part, axis=0, keepdims=True)
        for i in range(2):
            rows_ref[12 + i : 13 + i, :] += gain_row[:, 128 * i : 128 * i + 128]
            rows_ref[14 + i : 15 + i, :] += shift_row[:, 128 * i : 128 * i + 128]
        return part

    return pl.run_scoped(
        heads,
        *[pltpu.VMEM((128, tokens), BF16)] * 3,
        *[pltpu.VMEM((tokens, 256), BF16)] * 2,
        *[pltpu.VMEM((128, tokens), F32)] * 3,
    )


def feed_forward(x, att, top, w_ref, base, vec_ref, n2_ref, acc_ref, gn_ref, gp_ref, g1_ref, g2_ref, rows_ref):
    middle = x + mm(att, w_ref[base : base + 256, :]) + vec_ref[4:5]
    unit, inverse = unit_rows(middle)
    n2_ref[...] = (unit * vec_ref[5:6] + vec_ref[6:7]).astype(BF16)
    acc_ref[...] = middle + vec_ref[11:12]
    gn_ref[...] = jnp.zeros_like(gn_ref)
    for f in range(4):
        w1 = w_ref[base + 256 * (1 + f) : base + 256 * (2 + f), :]
        w2 = w_ref[base + 256 * (5 + f) : base + 256 * (6 + f), :]
        cols = slice(256 * f, 256 * f + 256)
        hidden = mm(n2_ref[...], w1) + vec_ref[7 + f : 8 + f]
        below = 0.5 * (1.0 + lax.erf(hidden * (0.5**0.5)))
        active = (hidden * below).astype(BF16)
        slope = below + hidden * jnp.exp(-0.5 * hidden * hidden) * 0.3989422804014327
        grad_hidden = (mm_nt(top, w2) * slope).astype(BF16)
        acc_ref[...] += mm(active, w2)
        gn_ref[...] += mm_nt(grad_hidden, w1)
        g1_ref[:, cols] += mm_tn(n2_ref[...], grad_hidden)
        g2_ref[:, cols] += mm_tn(top, active)
        rows_ref[3 + f : 4 + f, :] += jnp.sum(grad_hidden.astype(F32), axis=0, keepdims=True)
    grad_normed = gn_ref[...]
    top_f = top.astype(F32)
    grad_middle = top_f + norm_back(grad_normed, vec_ref[5:6], unit, inverse)
    branch = grad_middle.astype(BF16)
    gp_ref[...] += mm_tn(branch, att)
    rows_ref[0:1, :] += jnp.sum(branch.astype(F32), axis=0, keepdims=True)
    rows_ref[1:2, :] += jnp.sum(grad_normed * unit, axis=0, keepdims=True)
    rows_ref[2:3, :] += jnp.sum(grad_normed, axis=0, keepdims=True)
    rows_ref[7:8, :] += jnp.sum(top_f, axis=0, keepdims=True)
    grad_att = mm_nt(branch, w_ref[base : base + 256, :]).astype(BF16)
    return acc_ref[...].astype(BF16), grad_middle, grad_att


PARAMS = pltpu.CompilerParams(
    dimension_semantics=("arbitrary",), vmem_limit_bytes=VMEM_LIMIT
)


def whole(shape):
    return pl.BlockSpec(shape, lambda m: (0,) * len(shape))


def each(shape):
    return pl.BlockSpec((None,) + shape, lambda m: (m,) + (0,) * len(shape))


def shape_of(dtype, *shape):
    return jax.ShapeDtypeStruct(shape, dtype)


def pack_tokens(x, nb, length):
    micro, tokens, channels = x.shape

    def kernel(x_ref, o_ref, hot):
        @pl.when(pl.program_id(0) == 0)
        def _():
            hot[...] = order_out(nb, length)

        o_ref[...] = mm(hot[...], x_ref[...]).astype(BF16)

    return pl.pallas_call(
        kernel,
        grid=(micro,),
        in_specs=[each((tokens, channels))],
        out_specs=each((nb * PIECE, channels)),
        out_shape=shape_of(BF16, micro, nb * PIECE, channels),
        scratch_shapes=[pltpu.VMEM((nb * PIECE, tokens), BF16)],
        compiler_params=PARAMS,
        name="pack_tokens",
    )(x)


def forward_call(x, half, nb, length, weights, vectors):
    micro = x.shape[0]
    tokens = STRIPE * length
    packed = nb * PIECE

    def kernel(x_ref, w_ref, vec_ref, qa_ref, k_ref, v_ref, o_ref, att_ref, xs_ref, *scr):
        if half == 0:
            attention_forward(
                x_ref[...].astype(F32), half_rows(vec_ref, half), length, lane_blocks(w_ref, half), vec_ref, qa_ref, k_ref, v_ref, o_ref, att_ref
            )
        else:
            att_s, hot_in, hot_out = scr

            @pl.when(pl.program_id(0) == 0)
            def _():
                hot_in[...] = order_in(nb, length)
                hot_out[...] = order_out(nb, length)

            xs_ref[...] = mm(hot_in[...], x_ref[...]).astype(BF16)
            attention_forward(
                xs_ref[...].astype(F32), half_rows(vec_ref, half), length, lane_blocks(w_ref, half), vec_ref, qa_ref, k_ref, v_ref, o_ref, att_s
            )
            att_ref[...] = mm(hot_out[...], att_s[...]).astype(BF16)

    rows = tokens if half == 0 else packed
    scratch = []
    if half == 1:
        scratch += [
            pltpu.VMEM((tokens, 128), BF16),
            pltpu.VMEM((tokens, packed), BF16),
            pltpu.VMEM((packed, tokens), BF16),
        ]
    if half == 0:
        def body(x_ref, w_ref, vec_ref, qa_ref, k_ref, v_ref, o_ref, att_ref, *scr):
            kernel(x_ref, w_ref, vec_ref, qa_ref, k_ref, v_ref, o_ref, att_ref, None, *scr)
        extra_specs, extra_shapes = [], []
    else:
        body = kernel
        extra_specs = [each((tokens, 256))]
        extra_shapes = [shape_of(BF16, micro, tokens, 256)]
    return pl.pallas_call(
        body,
        grid=(micro,),
        in_specs=[each((rows, 256)), whole(weights.shape), whole(vectors.shape)],
        out_specs=[
            each((tokens, 256)),
            each((tokens, 128)),
            each((tokens, 128)),
            each((tokens, 128)),
            each((rows, 128)),
        ] + extra_specs,
        out_shape=[
            shape_of(BF16, micro, tokens, 256),
            shape_of(BF16, micro, tokens, 128),
            shape_of(BF16, micro, tokens, 128),
            shape_of(F32, micro, tokens, 128),
            shape_of(BF16, micro, rows, 128),
        ] + extra_shapes,
        scratch_shapes=scratch,
        compiler_params=PARAMS,
        name="attention_forward_%d" % half,
    )(x, weights, vectors)


def middle_call(x, att_h, att_v, top, nb, length, weights, vectors):
    micro, tokens, _ = x.shape
    packed = nb * PIECE

    def kernel(
        x_ref, h_ref, v_ref, top_ref, w_ref, vec_ref,
        out_ref, gm_ref, gh_ref, gv_ref, gp_ref, g1_ref, g2_ref, rows_ref,
        hot_in, hot_out, att, n2, acc, gn,
    ):
        @pl.when(pl.program_id(0) == 0)
        def _():
            hot_in[...] = order_in(nb, length)
            hot_out[...] = order_out(nb, length)
            for ref in (gp_ref, g1_ref, g2_ref, rows_ref):
                ref[...] = jnp.zeros_like(ref)

        att[:, 0:128] = h_ref[...]
        att[:, 128:256] = mm(hot_in[...], v_ref[...]).astype(BF16)
        out, grad_middle, grad_att = feed_forward(
            x_ref[...].astype(F32), att[...], top_ref[...], w_ref, ROW_PROJ, vec_ref, n2, acc, gn, gp_ref, g1_ref, g2_ref, rows_ref
        )
        out_ref[...] = out
        gm_ref[...] = grad_middle
        gh_ref[...] = grad_att[:, 0:128]
        gv_ref[...] = mm(hot_out[...], grad_att[:, 128:256]).astype(BF16)

    return pl.pallas_call(
        kernel,
        grid=(micro,),
        in_specs=[
            each((tokens, 256)), each((tokens, 128)), each((packed, 128)), each((tokens, 256)),
            whole(weights.shape), whole(vectors.shape),
        ],
        out_specs=[
            each((tokens, 256)), each((tokens, 256)), each((tokens, 128)), each((packed, 128)),
            whole((256, 256)), whole((256, 1024)), whole((256, 1024)), whole((8, 256)),
        ],
        out_shape=[
            shape_of(BF16, micro, tokens, 256), shape_of(F32, micro, tokens, 256),
            shape_of(BF16, micro, tokens, 128), shape_of(BF16, micro, packed, 128),
            shape_of(F32, 256, 256), shape_of(F32, 256, 1024), shape_of(F32, 256, 1024), shape_of(F32, 8, 256),
        ],
        scratch_shapes=[
            pltpu.VMEM((tokens, packed), BF16), pltpu.VMEM((packed, tokens), BF16),
            pltpu.VMEM((tokens, 256), BF16), pltpu.VMEM((tokens, 256), BF16),
            pltpu.VMEM((tokens, 256), F32), pltpu.VMEM((tokens, 256), F32),
        ],
        compiler_params=PARAMS,
        name="feed_forward",
    )(x, att_h, att_v, top, weights, vectors)


def backward_call(x, grad, qa, k, v, o, half, nb, length, weights, vectors):
    micro, tokens, _ = x.shape
    packed = nb * PIECE

    def kernel(
        x_ref, g_ref, qa_ref, k_ref, v_ref, o_ref, w_ref, vec_ref, gn_ref, gw_ref, rows_ref,
        da, *scr,
    ):
        @pl.when(pl.program_id(0) == 0)
        def _():
            gw_ref[...] = jnp.zeros_like(gw_ref)
            rows_ref[...] = jnp.zeros_like(rows_ref)
            if half == 1:
                scr[0][...] = order_in(nb, length)
                scr[1][...] = order_out(nb, length)

        grad_in = g_ref[...] if half == 0 else mm(scr[0][...], g_ref[...]).astype(BF16)
        part = attention_backward(
            x_ref[...].astype(F32), half_rows(vec_ref, half), length, grad_in, lane_blocks(w_ref, half), vec_ref, qa_ref, k_ref, v_ref, o_ref,
            da, gw_ref, rows_ref,
        )
        if half == 0:
            gn_ref[...] = part
        else:
            gn_ref[...] = mm(scr[1][...], part.astype(BF16)).astype(BF16)

    rows = tokens if half == 0 else packed
    scratch = [pltpu.VMEM((tokens, 256), BF16)]
    if half == 1:
        scratch += [pltpu.VMEM((tokens, packed), BF16), pltpu.VMEM((packed, tokens), BF16)]
    return pl.pallas_call(
        kernel,
        grid=(micro,),
        in_specs=[
            each((tokens, 256)), each((rows, 128)), each((tokens, 256)), each((tokens, 128)),
            each((tokens, 128)), each((tokens, 128)), whole(weights.shape), whole(vectors.shape),
        ],
        out_specs=[each((rows, 256)), whole((256, 384)), whole((16, 128))],
        out_shape=[
            shape_of(F32 if half == 0 else BF16, micro, rows, 256),
            shape_of(F32, 256, 384), shape_of(F32, 16, 128),
        ],
        scratch_shapes=scratch,
        compiler_params=PARAMS,
        name="attention_backward_%d" % half,
    )(x, grad, qa, k, v, o, weights, vectors)


def last_call(x, grad_middle, part_h, part_v, nb, length, vectors):
    micro, tokens, _ = x.shape
    packed = nb * PIECE

    def kernel(x_ref, gm_ref, h_ref, v_ref, vec_ref, out_ref, hot_in):
        @pl.when(pl.program_id(0) == 0)
        def _():
            hot_in[...] = order_in(nb, length)

        grad_normed = h_ref[...] + mm(hot_in[...], v_ref[...])
        unit, inverse = unit_rows(x_ref[...].astype(F32))
        out_ref[...] = (
            gm_ref[...] + norm_back(grad_normed, vec_ref[0:1], unit, inverse)
        ).astype(BF16)

    return pl.pallas_call(
        kernel,
        grid=(micro,),
        in_specs=[
            each((tokens, 256)), each((tokens, 256)), each((tokens, 256)), each((packed, 256)), whole(vectors.shape),
        ],
        out_specs=each((tokens, 256)),
        out_shape=shape_of(BF16, micro, tokens, 256),
        scratch_shapes=[pltpu.VMEM((tokens, packed), BF16)],
        compiler_params=PARAMS,
        name="input_gradient",
    )(x, grad_middle, part_h, part_v, vectors)


def repeat(lo, hi, body):
    def step(k, c):
        body(k)
        return c

    lax.fori_loop(lo, hi, step, 0)


def remote(src, dst, ss, rs, dev):
    return pltpu.make_async_remote_copy(
        src_ref=src, dst_ref=dst, send_sem=ss, recv_sem=rs, device_id=dev, device_id_type=MESH
    )


def await_bytes(ref, sem):
    pltpu.make_async_copy(ref, ref, sem).wait()


class Swap:
    def __init__(self, n, out_ref, in_ref, send_sem, recv_sem):
        self.n, self.out, self.into, self.ss, self.rs = n, out_ref, in_ref, send_sem, recv_sem
        self.me = lax.axis_index("band")

    def rows(self, i):
        return pl.ds(pl.multiple_of(i * PIECE, PIECE), PIECE)

    def send(self, m):
        mine = self.rows(self.me)

        def one(k):
            d = lax.rem(self.me + k, self.n)
            remote(
                self.out.at[m, self.rows(d)],
                self.into.at[m, mine],
                self.ss.at[m],
                self.rs.at[m],
                {"band": d},
            ).start()

        repeat(1, self.n, one)
        self.into[m, mine, :] = self.out[m, mine, :]

    def wait(self, m):
        others = pl.ds(0, (self.n - 1) * PIECE)
        await_bytes(self.out.at[m, others], self.ss.at[m])
        await_bytes(self.into.at[m, others], self.rs.at[m])


class Sum:
    def __init__(self, nb, nx, x_ref, o_ref, got, half, recv, sems):
        self.nx = nx
        self.nq = (nb // 2) * nx
        self.p = x_ref.shape[0] // (2 * self.nq)
        band = lax.axis_index("band")
        self.core = lax.rem(band, 2)
        self.q = (band // 2) * nx + lax.axis_index("batch")
        self.sibling = {"band": band + 1 - 2 * self.core}
        self.x, self.o, self.got, self.half, self.recv = x_ref, o_ref, got, half, recv
        self.sems = sems

    def chip(self, t):
        return {"band": (t // self.nx) * 2 + self.core, "batch": lax.rem(t, self.nx)}

    def ahead(self, k):
        return lax.rem(self.q + k, self.nq)

    def behind(self, k):
        return lax.rem(self.q - k + self.nq, self.nq)

    def side(self, c):
        rows = self.nq * self.p
        return pl.ds(pl.multiple_of(c * rows, 16), rows)

    def wide(self, c, t):
        return pl.ds(pl.multiple_of((c * self.nq + t) * self.p, 16), self.p)

    def thin(self, t):
        return pl.ds(pl.multiple_of(t * self.p, 16), self.p)

    def sem(self, i):
        return self.sems.at[2 * i], self.sems.at[2 * i + 1]

    def arrived(self, i, sent, came):
        await_bytes(sent, self.sems.at[2 * i])
        await_bytes(came, self.sems.at[2 * i + 1])

    def pair_copy(self, c):
        return remote(self.x.at[self.side(c)], self.got, *self.sem(0), self.sibling)

    def start(self):
        self.pair_copy(1 - self.core).start()

    def scatter(self):
        self.pair_copy(self.core).wait()
        self.half[...] = (
            self.x[self.side(self.core)].astype(F32) + self.got[...].astype(F32)
        ).astype(BF16)

        def one(k):
            t = self.ahead(k)
            remote(
                self.half.at[self.thin(t)],
                self.recv.at[self.thin(self.q)],
                *self.sem(1),
                self.chip(t),
            ).start()

        repeat(1, self.nq, one)
        self.recv[self.thin(self.q)] = self.half[self.thin(self.q)]

    def gather(self):
        others = pl.ds(0, (self.nq - 1) * self.p)
        self.arrived(1, self.half.at[others], self.recv.at[others])
        total = self.recv[0 : self.p].astype(F32)
        for t in range(1, self.nq):
            total = total + self.recv[t * self.p : (t + 1) * self.p].astype(F32)
        mine = self.wide(self.core, self.q)
        self.o[mine] = total.astype(BF16)

        def give(k):
            remote(
                self.o.at[mine], self.o.at[mine], *self.sem(2), self.chip(self.ahead(k))
            ).start()

        repeat(1, self.nq, give)

    def pass_on(self, c):
        return remote(
            self.o.at[self.side(self.core)], self.o.at[self.side(c)], *self.sem(3), self.sibling
        )

    def relay(self):
        others = pl.ds(0, (self.nq - 1) * self.p)
        self.arrived(2, self.o.at[others], self.o.at[others])
        self.pass_on(self.core).start()

    def finish(self):
        self.pass_on(1 - self.core).wait()


class DeepSum:
    def __init__(self, nb, nx, x_ref, o_ref, got, half, recv, deep, deep_recv, sems):
        self.nx = nx
        self.n1, self.n2 = 2 * nx, nb // 4
        self.p = x_ref.shape[0] // (2 * self.n1 * self.n2)
        band = lax.axis_index("band")
        self.core = lax.rem(band, 2)
        self.j1 = lax.rem(band // 2, 2) * nx + lax.axis_index("batch")
        self.j2 = band // 4
        self.sibling = {"band": band + 1 - 2 * self.core}
        self.x, self.o, self.got, self.half, self.recv = x_ref, o_ref, got, half, recv
        self.deep, self.deep_recv = deep, deep_recv
        self.sems = sems

    def near(self, t):
        return {
            "band": self.j2 * 4 + (t // self.nx) * 2 + self.core,
            "batch": lax.rem(t, self.nx),
        }

    def far(self, t):
        return {"band": t * 4 + lax.rem(lax.axis_index("band"), 4)}

    def near_at(self, k):
        return lax.rem(self.j1 + k, self.n1)

    def far_at(self, k):
        return lax.rem(self.j2 + k, self.n2)

    def block(self, c, t):
        rows = self.n2 * self.p
        return pl.ds(pl.multiple_of((c * self.n1 + t) * rows, 16), rows)

    def thin(self, t):
        rows = self.n2 * self.p
        return pl.ds(pl.multiple_of(t * rows, 16), rows)

    def piece(self, t):
        return pl.ds(pl.multiple_of(t * self.p, 16), self.p)

    def o_piece(self, t):
        at = (self.core * self.n1 + self.j1) * self.n2 + t
        return self.o.at[pl.ds(pl.multiple_of(at * self.p, 16), self.p)]

    def sem(self, i):
        return self.sems.at[2 * i], self.sems.at[2 * i + 1]

    def arrived(self, i, sent, came):
        await_bytes(sent, self.sems.at[2 * i])
        await_bytes(came, self.sems.at[2 * i + 1])

    def side(self, c):
        rows = self.n1 * self.n2 * self.p
        return pl.ds(pl.multiple_of(c * rows, 16), rows)

    def pair_copy(self, c):
        return remote(self.x.at[self.side(c)], self.got, *self.sem(0), self.sibling)

    def start(self):
        self.pair_copy(1 - self.core).start()

    def scatter(self):
        self.pair_copy(self.core).wait()
        self.half[...] = (
            self.x[self.side(self.core)].astype(F32) + self.got[...].astype(F32)
        ).astype(BF16)

        def one(k):
            t = self.near_at(k)
            remote(
                self.half.at[self.thin(t)],
                self.recv.at[self.thin(self.j1)],
                *self.sem(1),
                self.near(t),
            ).start()

        repeat(1, self.n1, one)

    def scatter_far(self):
        others = pl.ds(0, (self.n1 - 1) * self.n2 * self.p)
        self.arrived(1, self.half.at[others], self.recv.at[others])
        total = self.half[self.thin(self.j1)].astype(F32)
        for k in range(1, self.n1):
            total = total + self.recv[self.thin(self.near_at(k))].astype(F32)
        self.deep[...] = total.astype(BF16)

        def give(k):
            t = self.far_at(k)
            remote(
                self.deep.at[self.piece(t)],
                self.deep_recv.at[self.piece(self.j2)],
                *self.sem(2),
                self.far(t),
            ).start()

        repeat(1, self.n2, give)

    def gather(self):
        others = pl.ds(0, (self.n2 - 1) * self.p)
        self.arrived(2, self.deep.at[others], self.deep_recv.at[others])
        total = self.deep[self.piece(self.j2)].astype(F32)
        for k in range(1, self.n2):
            total = total + self.deep_recv[self.piece(self.far_at(k))].astype(F32)
        at = (self.core * self.n1 + self.j1) * self.n2 + self.j2
        self.o[pl.ds(pl.multiple_of(at * self.p, 16), self.p)] = total.astype(BF16)
        mine = self.o_piece(self.j2)
        repeat(
            1,
            self.n2,
            lambda k: remote(mine, mine, *self.sem(3), self.far(self.far_at(k))).start(),
        )

    def gather_near(self):
        others = pl.ds(0, (self.n2 - 1) * self.p)
        self.arrived(3, self.o.at[others], self.o.at[others])
        mine = self.o.at[self.block(self.core, self.j1)]
        repeat(
            1,
            self.n1,
            lambda k: remote(mine, mine, *self.sem(4), self.near(self.near_at(k))).start(),
        )

    def pass_on(self, c):
        return remote(
            self.o.at[self.side(self.core)], self.o.at[self.side(c)], *self.sem(5), self.sibling
        )

    def relay(self):
        others = pl.ds(0, (self.n1 - 1) * self.n2 * self.p)
        self.arrived(4, self.o.at[others], self.o.at[others])
        self.pass_on(self.core).start()

    def finish(self):
        self.pass_on(1 - self.core).wait()


ROWS_A = 1536
ROWS_B = 2304
ROWS_G = 800


def up(rows, unit):
    return -(-rows // unit) * unit


def split_rows(ref, at, rows):
    n = rows.shape[0]
    high = rows.astype(BF16)
    ref[at : at + n, :] = high
    ref[at + n : at + 2 * n, :] = (rows - high.astype(F32)).astype(BF16)


def block_kernel(
    nb, nx, length,
    own_ref, x_ref, wq_ref, vec_ref, top_hbm, wp_hbm, w1_hbm, w2_hbm,
    out_ref, ing_ref, gb_ref, gav_ref, gah_ref,
    wa_in, wb_in, wa, wb, gb_in, gav_in, gah_in,
    wide_got, wide_half, wide_recv, wide_deep, wide_deep_recv,
    a_got, a_half, a_recv, a_deep, a_deep_recv,
    gb_got, gb_half, gb_recv, gb_deep, gb_deep_recv,
    v_got, v_half, v_recv, v_deep, v_deep_recv, h_got, h_half, h_recv,
    hot_in, hot_out, x_out, x_in, a_out, a_in, g_in, p_in,
    xs, qa, ks, vs, os, att_w, att, n2, acc, gn, gm, grad_w, part_w, hv_ref,
    gp, g1, g2, rows_mid, gw, rows, da,
    x_ss, x_rs, a_ss, a_rs, g_ss, g_rs, p_ss, p_rs,
    wa_sem, wb_sem, gb_sem, gav_sem, gah_sem,
    top_ref, wp_ref, w1_ref, w2_ref, fetch_sem,
):
    fetches = [
        pltpu.make_async_copy(src, dst, fetch_sem.at[i])
        for i, (src, dst) in enumerate(
            ((wp_hbm, wp_ref), (w1_hbm, w1_ref), (w2_hbm, w2_ref), (top_hbm, top_ref))
        )
    ]
    for c in fetches:
        c.start()
    band = lax.axis_index("band")
    batch = lax.axis_index("batch")
    device = band * nx + batch
    micro = x_ref.shape[0]
    core = lax.rem(band, 2)
    bar = pltpu.get_barrier_semaphore()
    repeat(
        1,
        nb,
        lambda k: pl.semaphore_signal(
            bar, inc=1, device_id={"band": lax.rem(band + k, nb)}, device_id_type=MESH
        ),
    )

    def greet(t):
        other = lax.rem(batch + 1 + t // (nb // 2), nx)
        pl.semaphore_signal(
            bar,
            inc=1,
            device_id={"band": lax.rem(t, nb // 2) * 2 + core, "batch": other},
            device_id_type=MESH,
        )

    repeat(0, (nb // 2) * (nx - 1), greet)

    sum_wa = DeepSum(
        nb, nx, wa_in, wa, a_got, a_half, a_recv, a_deep, a_deep_recv, wa_sem
    )
    sum_wb = DeepSum(
        nb, nx, wb_in, wb, wide_got, wide_half, wide_recv, wide_deep, wide_deep_recv, wb_sem
    )
    sum_gb = DeepSum(
        nb, nx, gb_in, gb_ref, gb_got, gb_half, gb_recv, gb_deep, gb_deep_recv, gb_sem
    )
    sum_gav = DeepSum(
        nb, nx, gav_in, gav_ref, v_got, v_half, v_recv, v_deep, v_deep_recv, gav_sem
    )
    sum_gah = Sum(nb, nx, gah_in, gah_ref, h_got, h_half, h_recv, gah_sem)
    swap_x = Swap(nb, x_out, x_in, x_ss, x_rs)
    swap_a = Swap(nb, a_out, a_in, a_ss, a_rs)
    swap_g = Swap(nb, a_out, g_in, g_ss, g_rs)
    swap_p = Swap(nb, x_out, p_in, p_ss, p_rs)

    def own(ref, which, cols):
        return jnp.where(own_ref[which] == device, ref[0, :, cols], 0.0).astype(BF16)

    for b in range(6):
        wa_in[256 * b : 256 * b + 256, :] = own(wq_ref, 0, slice(128 * b, 128 * b + 128))
    if wa_in.shape[0] > ROWS_A:
        wa_in[ROWS_A:, :] = jnp.zeros((wa_in.shape[0] - ROWS_A, 128), BF16)
    pl.semaphore_wait(bar, nb - 1 + (nb // 2) * (nx - 1))
    sum_wa.start()
    sum_wa.scatter()
    for c in fetches[:3]:
        c.wait()
    wb_in[0:256, :] = own(wp_ref, 1, slice(0, 256))
    for f in range(4):
        wb_in[256 * (f + 1) : 256 * (f + 2), :] = own(w1_ref, 2, slice(256 * f, 256 * f + 256))
    wb_in[1280:ROWS_B, :] = own(w2_ref, 3, slice(0, 256))
    wb_in[ROWS_B:, :] = jnp.zeros((wb_in.shape[0] - ROWS_B, 256), BF16)
    sum_wb.start()
    hot_out[...] = order_out(nb, length)
    x_out[0] = mm(hot_out[...], x_ref[0]).astype(BF16)
    sum_wa.scatter_far()
    swap_x.send(0)
    sum_wb.scatter()
    sum_wa.gather()
    hot_in[...] = order_in(nb, length)
    for m in range(1, micro):
        x_out[m] = mm(hot_out[...], x_ref[m]).astype(BF16)
    sum_wa.gather_near()
    for m in range(1, micro):
        swap_x.send(m)
    sum_wa.relay()
    for ref in (gp, g1, g2, rows_mid, gw, rows):
        ref[...] = jnp.zeros_like(ref)
    for half in range(2):
        get = half_rows(vec_ref, half)
        for i in range(12):
            hv_ref[half, i : i + 1, :] = get(i)
    for m in range(micro):
        xs[m] = x_ref[m]
    sum_wa.finish()

    def blocks(half):
        return lambda b: wa[pl.ds(pl.multiple_of(256 * (2 * b + half), 256), 256), :]

    def vectors_of(half):
        return lambda i: hv_ref[half, i : i + 1, :]

    def forward_step(w):
        half, m = w // micro, lax.rem(w, micro)

        @pl.when(w >= micro)
        def _():
            swap_x.wait(m)
            xs[w] = mm(hot_in[...], x_in[m]).astype(BF16)

        attention_forward(
            xs[w].astype(F32), vectors_of(half), length, blocks(half), vec_ref,
            qa.at[w], ks.at[w], vs.at[w], os.at[w], att_w.at[w],
        )

        @pl.when(w >= micro)
        def _():
            a_out[m] = mm(hot_out[...], att_w[w]).astype(BF16)
            swap_a.send(m)

        pl.when(w == 0)(sum_wb.scatter_far)
        pl.when(w == micro - 1)(sum_wb.gather)
        pl.when(w == micro)(sum_wb.gather_near)

    repeat(0, 2 * micro, forward_step)
    sum_wb.relay()
    sum_wb.finish()
    fetches[3].wait()

    def middle_step(m):
        swap_a.wait(m)
        att[:, 0:128] = att_w[m]
        att[:, 128:256] = mm(hot_in[...], a_in[m]).astype(BF16)
        out, grad_middle, grad_att = feed_forward(
            x_ref[m].astype(F32), att[...], top_ref[m], wb, 0, vec_ref, n2, acc, gn,
            gp, g1, g2, rows_mid,
        )
        out_ref[m] = out
        gm[m] = grad_middle
        grad_w[m] = grad_att[:, 0:128]
        a_out[m] = mm(hot_out[...], grad_att[:, 128:256]).astype(BF16)
        swap_g.send(m)

    repeat(0, micro, middle_step)
    gb_in[0:256, :] = jnp.transpose(gp[...]).astype(BF16)
    for f in range(4):
        cols = slice(256 * f, 256 * f + 256)
        gb_in[256 * (f + 1) : 256 * (f + 2), :] = g1[:, cols].astype(BF16)
        gb_in[1280 + 256 * f : 1536 + 256 * f, :] = jnp.transpose(g2[:, cols]).astype(BF16)
    gb_in[ROWS_B:, :] = jnp.zeros((gb_in.shape[0] - ROWS_B, 256), BF16)
    split_rows(gb_in, ROWS_B, rows_mid[...])
    sum_gb.start()

    def fill(ref, half):
        for b in range(3):
            ref[256 * b : 256 * b + 256, :] = gw[half, :, 128 * b : 128 * b + 128].astype(BF16)
        split_rows(ref, 768, rows[half])
        ref[ROWS_G:, :] = jnp.zeros((ref.shape[0] - ROWS_G, 128), BF16)

    def backward_step(i):
        w = lax.rem(i + micro, 2 * micro)
        half, m = w // micro, lax.rem(w, micro)

        @pl.when(w >= micro)
        def _():
            swap_g.wait(m)
            grad_w[w] = mm(hot_in[...], g_in[m]).astype(BF16)

        def between():
            pl.when(i == 0)(sum_gb.scatter)
            pl.when(i == micro - 1)(sum_gb.scatter_far)

            @pl.when(i == micro)
            def _():
                sum_gb.gather()
                sum_gav.scatter()

            @pl.when(i == 2 * micro - 1)
            def _():
                sum_gb.gather_near()
                sum_gav.gather()

        into = jnp.where(w >= micro, micro, m)
        part_w[into] = attention_backward(
            xs[w].astype(F32), vectors_of(half), length, grad_w[w], blocks(half), vec_ref,
            qa.at[w], ks.at[w], vs.at[w], os.at[w], da, gw.at[half], rows.at[half],
            between,
        )

        @pl.when(w >= micro)
        def _():
            x_out[m] = mm(hot_out[...], part_w[micro].astype(BF16)).astype(BF16)
            swap_p.send(m)

        @pl.when(i == micro - 1)
        def _():
            fill(gav_in, 1)
            sum_gav.start()

        pl.when(i == micro)(sum_gav.scatter_far)

    repeat(0, 2 * micro, backward_step)
    fill(gah_in, 0)
    sum_gah.start()
    sum_gav.gather_near()
    sum_gah.scatter()
    sum_gb.relay()

    def last_step(m):
        swap_p.wait(m)
        grad_normed = part_w[m] + mm(hot_in[...], p_in[m])
        unit, inverse = unit_rows(x_ref[m].astype(F32))
        ing_ref[m] = (gm[m] + norm_back(grad_normed, vec_ref[0:1], unit, inverse)).astype(BF16)

    last_step(0)
    sum_gah.gather()
    sum_gav.relay()
    repeat(1, micro, last_step)
    sum_gah.relay()
    sum_gb.finish()
    sum_gav.finish()
    sum_gah.finish()


def block_call(x, top, owners, w_qkv, w_proj, w_fc1, w_fc2, vectors, nb, nx, length):
    micro, tokens, _ = x.shape
    packed = nb * PIECE
    nq = nb // 2 * nx
    unit = 32 * nq
    ra, rb, rg = up(ROWS_A, unit), up(ROWS_B + 16, unit), up(ROWS_G, unit)
    vm = pltpu.VMEM
    windows = 2 * micro

    def steps(rows, cols):
        return [vm((rows // 2, cols), BF16)] * 3

    def deep_steps(rows, cols):
        return steps(rows, cols) + [vm((rows // (4 * nx), cols), BF16)] * 2

    scratch = (
        [vm((ra, 128), BF16), vm((rb, 256), BF16), vm((ra, 128), BF16), vm((rb, 256), BF16)]
        + [vm((rb, 256), BF16), vm((rg, 128), BF16), vm((rg, 128), BF16)]
        + deep_steps(rb, 256) + deep_steps(ra, 128) + deep_steps(rb, 256) + deep_steps(rg, 128)
        + steps(rg, 128)
        + [vm((tokens, packed), BF16), vm((packed, tokens), BF16)]
        + [vm((micro, packed, 256), BF16)] * 2
        + [vm((micro, packed, 128), BF16)] * 3
        + [vm((micro, packed, 256), BF16)]
        + [
            vm((windows, tokens, 256), BF16),
            vm((windows, tokens, 256), BF16),
            vm((windows, tokens, 128), BF16),
            vm((windows, tokens, 128), BF16),
            vm((windows, tokens, 128), F32),
            vm((windows, tokens, 128), BF16),
            vm((tokens, 256), BF16),
            vm((tokens, 256), BF16),
            vm((tokens, 256), F32),
            vm((tokens, 256), F32),
            vm((micro, tokens, 256), F32),
            vm((windows, tokens, 128), BF16),
            vm((micro + 1, tokens, 256), F32),
            vm((2, 16, 128), F32),
            vm((256, 256), F32),
            vm((256, 1024), F32),
            vm((256, 1024), F32),
            vm((8, 256), F32),
            vm((2, 256, 384), F32),
            vm((2, 16, 128), F32),
            vm((tokens, 256), BF16),
        ]
        + [pltpu.SemaphoreType.DMA((micro,))] * 8
        + [pltpu.SemaphoreType.DMA((k,)) for k in (12, 12, 12, 12, 8)]
        + [vm(top.shape, BF16)]
        + [vm(w.shape, F32) for w in (w_proj, w_fc1, w_fc2)]
        + [pltpu.SemaphoreType.DMA((4,))]
    )
    whole_vmem = pl.BlockSpec(memory_space=vm)
    return pl.pallas_call(
        functools.partial(block_kernel, nb, nx, length),
        in_specs=[pl.BlockSpec(memory_space=pltpu.SMEM)]
        + [whole_vmem] * 3
        + [pl.BlockSpec(memory_space=pl.ANY)] * 4,
        out_specs=[whole_vmem] * 5,
        out_shape=[
            shape_of(BF16, micro, tokens, 256), shape_of(BF16, micro, tokens, 256),
            shape_of(BF16, rb, 256), shape_of(BF16, rg, 128), shape_of(BF16, rg, 128),
        ],
        scratch_shapes=scratch,
        compiler_params=pltpu.CompilerParams(
            collective_id=0, has_side_effects=True, vmem_limit_bytes=VMEM_LIMIT
        ),
        name="block",
    )(owners, x, w_qkv, vectors, top, w_proj, w_fc1, w_fc2)


def adam_kernel(
    own_ref, gb_ref, gav_ref, gah_ref, vec_ref, vf_ref, vs_ref, *refs,
):
    through = refs[0:2]
    moments = refs[2:14]
    bases = refs[14:22]
    grads_hbm = refs[22:26]
    outs = refs[26:38]
    vg_ref, vfn_ref, vsn_ref, vn_ref = refs[38:42]
    through_out = refs[42:44]
    held = refs[44:56]
    left = refs[56:64]
    grads = refs[64:68]
    zeros_ref, in_sem, out_sem, grad_sem, through_sem = refs[68:73]
    device = lax.axis_index("band") * lax.axis_size("batch") + lax.axis_index("batch")
    is_own = [own_ref[i] == device for i in range(4)]
    any_own = is_own[0] | is_own[1] | is_own[2] | is_own[3]

    def load(i):
        pairs = [(moments[3 * i + j].at[0], held[3 * i + j], 5 * i + j) for j in range(3)]
        pairs += [(bases[2 * i + j], left[2 * i + j], 5 * i + 3 + j) for j in range(2)]
        return [pltpu.make_async_copy(a, b, in_sem.at[s]) for a, b, s in pairs]

    def store(i, j):
        at = 3 * i + j
        return pltpu.make_async_copy(held[at], outs[at].at[0], out_sem.at[at])

    def blank(i):
        copies = []
        for j in range(3):
            shape = outs[3 * i + j].shape
            copies.append(
                pltpu.make_async_copy(
                    zeros_ref.at[pl.ds(0, shape[1]), pl.ds(0, shape[2])],
                    outs[3 * i + j].at[0],
                    out_sem.at[3 * i + j],
                )
            )
        return copies

    def start_blanks():
        for i in range(4):
            @pl.when(jnp.logical_not(is_own[i]))
            def _():
                for c in blank(i):
                    c.start()

    for i in range(4):
        @pl.when(is_own[i])
        def _():
            for c in load(i):
                c.start()

    zeros_ref[...] = jnp.zeros_like(zeros_ref)
    pl.when(jnp.logical_not(any_own))(start_blanks)
    passing = [
        pltpu.make_async_copy(a, b, through_sem.at[i])
        for i, (a, b) in enumerate(zip(through, through_out))
    ]
    for c in passing:
        c.start()

    for b in range(3):
        for half, ref in ((0, gah_ref), (1, gav_ref)):
            at = 256 * b + 128 * half
            grads[0][:, at : at + 128] = ref[256 * b : 256 * b + 256, :].astype(F32)
    grads[1][...] = gb_ref[0:256, :].astype(F32)
    for f in range(4):
        grads[2][:, 256 * f : 256 * f + 256] = gb_ref[256 * (f + 1) : 256 * (f + 2), :].astype(F32)
    grads[3][...] = gb_ref[1280:ROWS_B, :].astype(F32)
    giving = [pltpu.make_async_copy(grads[i], grads_hbm[i], grad_sem.at[i]) for i in range(4)]
    for c in giving:
        c.start()

    mid = gb_ref[ROWS_B : ROWS_B + 8, :].astype(F32) + gb_ref[ROWS_B + 8 : ROWS_B + 16, :].astype(F32)
    side = [r[768:784, :].astype(F32) + r[784:800, :].astype(F32) for r in (gah_ref, gav_ref)]
    both = side[0] + side[1]
    for i in range(2):
        vg_ref[0:1, 128 * i : 128 * i + 128] = both[12 + i : 13 + i]
        vg_ref[1:2, 128 * i : 128 * i + 128] = both[14 + i : 15 + i]
        vg_ref[2:4, 128 * i : 128 * i + 128] = side[i][0:2]
        vg_ref[21:22, 128 * i : 128 * i + 128] = side[i][11:12]
        for t in range(9):
            row = 12 + (t if i == 0 else 3 * (t % 3) + t // 3)
            vg_ref[row : row + 1, 128 * i : 128 * i + 128] = side[i][2 + t : 3 + t]
    vg_ref[4:12, :] = mid
    grad = vg_ref[...]
    first_new = BETA_ONE * vf_ref[...] + (1.0 - BETA_ONE) * grad
    second_new = BETA_TWO * vs_ref[...] + (1.0 - BETA_TWO) * grad * grad
    vfn_ref[...] = first_new
    vsn_ref[...] = second_new
    vn_ref[...] = vec_ref[...] - RATE_VECTORS * (first_new / (1.0 - BETA_ONE**STEP)) / (
        jnp.sqrt(second_new / (1.0 - BETA_TWO**STEP)) + EPS_ADAM
    )

    for i in range(4):
        @pl.when(is_own[i])
        def _():
            for c in load(i):
                c.wait()

    pl.when(any_own)(start_blanks)

    for i in range(4):
        @pl.when(is_own[i])
        def _():
            first, second, weight = held[3 * i], held[3 * i + 1], held[3 * i + 2]
            g = grads[i][...].astype(BF16)
            lh, rh = left[2 * i][...].astype(BF16), left[2 * i + 1][...].astype(BF16)
            once = jnp.transpose(mm_tn(g, lh)) if i == 3 else mm_tn(lh, g)
            turned_grad = mm(once.astype(BF16), rh)
            first_new = BETA_ONE * first[...] + (1.0 - BETA_ONE) * turned_grad
            second_new = BETA_TWO * second[...] + (1.0 - BETA_TWO) * turned_grad * turned_grad
            first[...] = first_new
            second[...] = second_new
            store(i, 0).start()
            store(i, 1).start()
            step = (first_new / (1.0 - BETA_ONE**STEP)) / (
                jnp.sqrt(second_new / (1.0 - BETA_TWO**STEP)) + EPS_ADAM
            )
            back = mm_nt(mm(lh, step.astype(BF16)).astype(BF16), rh)
            weight[...] = weight[...] - RATE * back - RATE * DECAY * weight[...]
            store(i, 2).start()

    for c in giving + passing:
        c.wait()
    for i in range(4):
        for j in range(3):
            store(i, j).wait()


def adam_call(
    owners, gb, gav, gah, vectors, vectors_first, vectors_second, through, slots, bases
):
    vm = pltpu.VMEM
    any_space = pl.BlockSpec(memory_space=pl.ANY)
    vspec = pl.BlockSpec(memory_space=vm)
    sizes = [(s.shape[1], s.shape[2]) for s in slots[::3]]
    vshape = shape_of(F32, *vectors.shape)
    tallest = max(a for a, _ in sizes)
    widest = max(b for _, b in sizes)
    dma = pltpu.SemaphoreType.DMA
    return pl.pallas_call(
        adam_kernel,
        in_specs=[pl.BlockSpec(memory_space=pltpu.SMEM)] + [vspec] * 8 + [any_space] * 20,
        out_specs=[any_space] * 16 + [vspec] * 4 + [any_space] * 2,
        out_shape=[shape_of(F32, *s) for s in sizes]
        + [shape_of(F32, *s.shape) for s in slots]
        + [vshape] * 4
        + [shape_of(t.dtype, *t.shape) for t in through],
        scratch_shapes=[vm((s.shape[1], s.shape[2]), F32) for s in slots]
        + [vm(b.shape, F32) for b in bases]
        + [vm(s, F32) for s in sizes]
        + [vm((tallest, widest), F32), dma((20,)), dma((12,)), dma((4,)), dma((2,))],
        compiler_params=pltpu.CompilerParams(vmem_limit_bytes=VMEM_LIMIT),
        name="adam",
    )(owners, gb, gav, gah, vectors, vectors_first, vectors_second, *through, *slots, *bases)


def wide_to_stack(w):
    n = w.shape[1] // 256
    return w.reshape(256, n, 256).transpose(1, 0, 2).reshape(256 * n, 256)


def by_steps(x, top, owners, slots, vectors, nb, nx, length):
    device_index = lax.axis_index(("band", "batch"))

    def own(slot, which):
        return jnp.where(device_index == owners[which], slot[0], 0.0).astype(BF16)

    stacked = jnp.concatenate(
        [
            wide_to_stack(own(slots[0], 0)),
            own(slots[1], 1),
            wide_to_stack(own(slots[2], 2)),
            own(slots[3], 3),
        ],
        axis=0,
    )
    weights = sum_everywhere(stacked, nb, nx, 0)[:ROW_END]

    def swap(packed, cid):
        m, rows, ch = packed.shape
        swapped = packed.reshape(m, nb, PIECE, ch).transpose(1, 0, 2, 3).reshape(m * rows, ch)
        got = exchange(swapped, nb, cid)
        return got.reshape(nb, m, PIECE, ch).transpose(1, 0, 2, 3).reshape(m, rows, ch)

    columns = swap(pack_tokens(x, nb, length), 1)
    qa_v, k_v, v_v, o_v, att_v, x_v = forward_call(columns, 1, nb, length, weights, vectors)
    qa_h, k_h, v_h, o_h, att_h = forward_call(x, 0, nb, length, weights, vectors)
    att_v = swap(att_v, 2)
    block_out, grad_middle, grad_h, grad_v, gp_t, g1, g2_t, rows_mid = middle_call(
        x, att_h, att_v, top, nb, length, weights, vectors
    )
    grad_v = swap(grad_v, 3)
    part_v, gw_v, rows_v = backward_call(
        x_v, grad_v, qa_v, k_v, v_v, o_v, 1, nb, length, weights, vectors
    )
    part_h, gw_h, rows_h = backward_call(
        x, grad_h, qa_h, k_h, v_h, o_h, 0, nb, length, weights, vectors
    )
    part_v = swap(part_v, 4)
    input_grad = last_call(x, grad_middle, part_h, part_v, nb, length, vectors)

    def two(rows):
        high = rows.astype(BF16)
        return [high, (rows - high.astype(F32)).astype(BF16)]

    gb = jnp.concatenate(
        [gp_t.T.astype(BF16), wide_to_stack(g1.astype(BF16)), g2_t.T.astype(BF16)] + two(rows_mid),
        axis=0,
    )

    def side(gw, rows):
        return jnp.concatenate(
            [gw[:, 128 * b : 128 * b + 128].astype(BF16) for b in range(3)] + two(rows), axis=0
        )

    gb = sum_everywhere(gb, nb, nx, 5)
    gav = sum_everywhere(side(gw_v, rows_v), nb, nx, 6)
    gah = sum_everywhere(side(gw_h, rows_h), nb, nx, 7)
    return block_out, input_grad, gb, gav, gah


def per_device(
    tokens_in, cotangent, owners,
    weight_qkv, weight_proj, weight_fc1, weight_fc2,
    first_qkv, second_qkv, first_proj, second_proj, first_fc1, second_fc1, first_fc2, second_fc2,
    left_qkv, right_qkv, left_proj, right_proj, left_fc1, right_fc1, left_fc2, right_fc2,
    vectors, vectors_first, vectors_second,
    *, nb, nx,
):
    micro, images, band_rows, length, channels = tokens_in.shape
    tokens = band_rows * length
    x = tokens_in.reshape(micro * images, tokens, channels)
    top = cotangent.reshape(micro * images, tokens, channels)
    weights = (weight_qkv, weight_proj, weight_fc1, weight_fc2)
    if tokens <= LONGEST:
        block_out, input_grad, gb, gav, gah = block_call(
            x, top, owners, *weights, vectors, nb, nx, length
        )
    else:
        block_out, input_grad, gb, gav, gah = by_steps(
            x, top, owners, weights, vectors, nb, nx, length
        )
    slots = (
        first_qkv, second_qkv, weight_qkv, first_proj, second_proj, weight_proj,
        first_fc1, second_fc1, weight_fc1, first_fc2, second_fc2, weight_fc2,
    )
    bases = (left_qkv, right_qkv, left_proj, right_proj, left_fc1, right_fc1, left_fc2, right_fc2)
    done = adam_call(
        owners, gb, gav, gah, vectors, vectors_first, vectors_second,
        (block_out, input_grad), slots, bases,
    )
    results = [done[20].reshape(tokens_in.shape), done[21].reshape(tokens_in.shape)]
    for i in range(4):
        results.append(done[i])
        results += list(done[4 + 3 * i : 7 + 3 * i])
    return tuple(results) + tuple(done[16:20])


def solution(mesh):
    tokens_spec = P(None, "batch", "band", None, None)
    slot_spec = P(("band", "batch"), None, None)
    return jax.shard_map(
        functools.partial(per_device, nb=mesh.shape["band"], nx=mesh.shape["batch"]),
        mesh=mesh,
        in_specs=(tokens_spec, tokens_spec, P()) + (slot_spec,) * 12 + (P(),) * 11,
        out_specs=(tokens_spec, tokens_spec)
        + (P(), slot_spec, slot_spec, slot_spec) * 4
        + (P(),) * 4,
        check_vma=False,
    )
```

profile of v0, /device:TPU:0, one launch (start us, length us, event | category | flops | bytes accessed | tf_op | source)
XLA Modules:
  0.0 158.1 jit_solution(12097610095120938104)
XLA Ops:
  0.7 146.2 %block.1 = (bf16[2,784,256]{2,1,0:T(8,128)(2,1)}, bf16[2,784,256]{2,1,0:T(8,128)(2,1)}, bf16[2560,256]{1,0:T(8,128)(2,1)}, bf16[1024,128]{1,0:T(8,128)(2,1)}, bf16[1024,128]{1,0:T(8,128)(2,1)}) custom-call(s32[4]{0:T(128)} %own_ref.3, bf16[2,784,256]{2,1,0:T(8,128)(2,1)} %bitcast.8, f32[1,256,768]{2,1,0:T(8,128)} %refs_4_.1, f32[22,256]{1,0:T(8,128)} %vec_ref.3, ...), custom_call_target="tpu_custom_call" | custom-call | tf_op jit(solution)/shard_map/block/pallas_call | solution.py:1295
  146.9 11.0 %adam.1 = (f32[256,768]{1,0:T(8,128)}, f32[256,256]{1,0:T(8,128)}, f32[256,1024]{1,0:T(8,128)}, f32[1024,256]{1,0:T(8,128)}, f32[1,256,768]{2,1,0:T(8,128)}, /*i...) custom-call(s32[4]{0:T(128)} %own_ref.3, ...), custom_call_target="tpu_custom_call" | custom-call | tf_op jit(solution)/shard_map/adam/pallas_call | solution.py:1455
where the time goes:
time: 159 us; the launch traced here: 158 us
  Pallas kernels  157 us (99%)
    pallas_call x1, Pallas kernels, block_call(): pl.pallas_call(functools.partial(block_kernel, nb, nx, length), in_specs=...  146 us
    pallas_call x1, Pallas kernels, adam_call(): pl.pallas_call(adam_kernel, in_specs=[pl.BlockSpec(memory_space=pltpu.SME...  11 us

commit v1 on v0

--- a/solution.py
+++ b/solution.py
@@ -336,7 +336,9 @@
     return lambda b: w_ref[256 * b : 256 * b + 256, 128 * half : 128 * half + 128]
 
 
-def attention_forward(x, hv, length, wb, vec_ref, qa_ref, k_ref, v_ref, o_ref, att_ref):
+def attention_forward(
+    x, hv, length, wb, vec_ref, qa_ref, k_ref, v_ref, o_ref, att_ref, between=None
+):
     tokens = x.shape[0]
     unit, _ = unit_rows(x)
     normed = (unit * vec_ref[0:1] + vec_ref[1:2]).astype(BF16)
@@ -365,6 +367,8 @@
             totals[rows, :] = both[HEAD_DIM:]
             tops[rows, :] = jnp.broadcast_to(highest, (HEAD_DIM, tokens))
 
+        if between is not None:
+            between()
         o_ref[...] = jnp.transpose(weighted[...] / totals[...])
         log_total = tops[...] + jnp.log2(totals[...])
         qa_ref[:, 128:256] = three_parts(-jnp.transpose(log_total))
@@ -1124,9 +1128,15 @@
             swap_x.wait(m)
             xs[w] = mm(hot_in[...], x_in[m]).astype(BF16)
 
+        def between():
+            pl.when(w == 0)(sum_wb.scatter_far)
+            pl.when(w == micro - 1)(sum_wb.gather)
+            pl.when(w == micro)(sum_wb.gather_near)
+            pl.when(w == 2 * micro - 1)(sum_wb.relay)
+
         attention_forward(
             xs[w].astype(F32), vectors_of(half), length, blocks(half), vec_ref,
-            qa.at[w], ks.at[w], vs.at[w], os.at[w], att_w.at[w],
+            qa.at[w], ks.at[w], vs.at[w], os.at[w], att_w.at[w], between,
         )
 
         @pl.when(w >= micro)
@@ -1134,12 +1144,7 @@
             a_out[m] = mm(hot_out[...], att_w[w]).astype(BF16)
             swap_a.send(m)
 
-        pl.when(w == 0)(sum_wb.scatter_far)
-        pl.when(w == micro - 1)(sum_wb.gather)
-        pl.when(w == micro)(sum_wb.gather_near)
-
     repeat(0, 2 * micro, forward_step)
-    sum_wb.relay()
     sum_wb.finish()
     fetches[3].wait()
 

time: 159 us -> 156 us (0.981)
  Pallas kernels: 157 us -> 155 us
    pallas_call x1, Pallas kernels: 146 us -> 144 us  [block_call(): pl.pallas_call(functools.partial(block_kernel, nb, nx, length), in_specs=...]
where the time goes in v1:
time: 156 us
  Pallas kernels  155 us (99%)
    pallas_call x1, Pallas kernels, block_call(): pl.pallas_call(functools.partial(block_kernel, nb, nx, length), in_specs=...  144 us
    pallas_call x1, Pallas kernels, adam_call(): pl.pallas_call(adam_kernel, in_specs=[pl.BlockSpec(memory_space=pltpu.SME...  11 us

profile of v1, /device:TPU:0, one launch (start us, length us, event | category | flops | bytes accessed | tf_op | source)
XLA Modules:
  0.0 155.8 jit_solution(9154424999437480213)
XLA Ops:
  0.7 144.0 %block.1 = (bf16[2,784,256]{2,1,0:T(8,128)(2,1)}, bf16[2,784,256]{2,1,0:T(8,128)(2,1)}, bf16[2560,256]{1,0:T(8,128)(2,1)}, bf16[1024,128]{1,0:T(8,128)(2,1)}, bf16[1024,128]{1,0:T(8,128)(2,1)}) custom-call(s32[4]{0:T(128)} %own_ref.3, bf16[2,784,256]{2,1,0:T(8,128)(2,1)} %bitcast.8, f32[1,256,768]{2,1,0:T(8,128)} %refs_4_.1, f32[22,256]{1,0:T(8,128)} %vec_ref.3, ...), custom_call_target="tpu_custom_call" | custom-call | tf_op jit(solution)/shard_map/block/pallas_call | solution.py:1300
  144.7 11.0 %adam.1 = (f32[256,768]{1,0:T(8,128)}, f32[256,256]{1,0:T(8,128)}, f32[256,1024]{1,0:T(8,128)}, f32[1024,256]{1,0:T(8,128)}, f32[1,256,768]{2,1,0:T(8,128)}, /*i...) custom-call(s32[4]{0:T(128)} %own_ref.3, ...), custom_call_target="tpu_custom_call" | custom-call | tf_op jit(solution)/shard_map/adam/pallas_call | solution.py:1460
